TPU v7x, 512 devices: a whole 4x4x16 slice. The times are simulated.
512 devices in a mesh: wide: 64 (over z, x_hi, core), narrow: 8 (over y, x_lo).
Axes of the slice: x: 4 (x_hi: 2, x_lo: 2; x = x_hi * 2 + x_lo), y: 4, z: 16, core: 2. Of those that a mesh axis runs over, the one named last changes fastest.
Arguments:
- panels: bfloat16 [64, 8192, 128], P('wide', 'narrow'), may hold values from -6 to 6
- stiff_blocks: bfloat16 [64, 1216, 4096], P('wide', 'narrow'), may hold values from -0.375 to 0.375
- mass_blocks: bfloat16 [64, 1216, 4096], P('wide', 'narrow'), may hold values from -0.375 to 0.375
- block_rows: int32 [64, 1216], P('wide', 'narrow'), may hold values from 0 to 16, as said below
- block_cols: int32 [64, 1216], P('wide', 'narrow'), may hold values from 0 to 127
- interface_map: int32 [64, 8192], P('wide', 'narrow'), may hold values from 0 to 8191, as said below
- cond_vectors: bfloat16 [8192, 768], P('narrow'), may hold values from -0.1875 to 0.1875
Outputs:
- condensed: bfloat16 [64, 8, 768, 512], P('wide', 'narrow')
Inputs may be any that keep to these rules, and one draw needn't show every extreme that they name: `block_rows`: in each partition's 152 slots the used slots come first; on some partition all 152 are used. `interface_map`: for every cell a permutation of the rows; of the 1024 rows of one partition at most 256 land in any one interface group, and in every cell some partition sends exactly 256 to some group.
All inputs are finite; a program needn't handle non-finite values.
Results may differ from a plain program's by a relative error of at most 0.0049.
Values may be sent and summed in bfloat16 or wider, within the bound.
A program may use at most 128 MiB of HBM per device.

v0:
```python
import jax
import jax.numpy as jnp
from jax import lax
from jax.sharding import PartitionSpec as P

BLK = 64
PC = 128
NC = 768
RB_DEV = 16
ROWS_DEV = 1024


def from_root(value, axis, source):
    kept = jnp.where(lax.axis_index(axis) == source, value, 0).astype(value.dtype)
    return lax.psum(kept, axis)


def body(panels, stiff_blocks, mass_blocks, block_rows, block_cols, interface_map, cond_vectors):
    group_count = lax.axis_size("narrow")
    cell_count = lax.axis_size("wide")
    slot_count = block_rows.shape[1]
    cell_blocks = RB_DEV * group_count
    peer_cap = 2 * ROWS_DEV // group_count
    stiffness = stiff_blocks.reshape(slot_count, BLK, BLK)
    mass_matrix = mass_blocks.reshape(slot_count, BLK, BLK)
    row_index = block_rows.reshape(slot_count)
    column_index = block_cols.reshape(slot_count)
    selector = (row_index[None, :] == jnp.arange(RB_DEV)[:, None]).astype(jnp.float32)
    owners = (0, cell_count // 2)
    panel_list = []
    for owner_index in owners:
        owner_rows = from_root(panels, "wide", owner_index)
        panel_list.append(lax.all_gather(owner_rows, "narrow", axis=1, tiled=True))
    pieces = []
    for panel_whole in panel_list:
        blocks = panel_whole.reshape(cell_blocks, BLK, PC)[column_index]
        for matrix in (stiffness, mass_matrix):
            product = jnp.einsum("sij,sjc->sic", matrix, blocks, preferred_element_type=jnp.float32)
            summed = jnp.einsum("rs,sic->ric", selector, product, precision=lax.Precision.HIGHEST)
            pieces.append(summed.reshape(ROWS_DEV, PC))
    product_rows = jnp.concatenate(pieces, axis=1).astype(jnp.bfloat16)
    position = interface_map.reshape(ROWS_DEV)
    target = position // ROWS_DEV
    slot_index = position % ROWS_DEV
    target_hits = (target[:, None] == jnp.arange(group_count)[None, :]).astype(jnp.int32)
    bucket_rank = jnp.sum(jnp.cumsum(target_hits, axis=0) * target_hits, axis=1) - 1
    send_rows = (
        jnp.zeros((group_count, peer_cap, 4 * PC), jnp.bfloat16)
        .at[target, bucket_rank]
        .set(product_rows)
    )
    send_slots = (
        jnp.full((group_count, peer_cap), ROWS_DEV, jnp.int32)
        .at[target, bucket_rank]
        .set(slot_index)
    )
    arrived, arrived_slots = (
        lax.all_to_all(send_rows, "narrow", split_axis=0, concat_axis=0, tiled=True),
        lax.all_to_all(send_slots, "narrow", split_axis=0, concat_axis=0, tiled=True),
    )
    placed = (
        jnp.zeros((ROWS_DEV, 4 * PC), jnp.bfloat16)
        .at[arrived_slots.reshape(-1)]
        .set(arrived.reshape(-1, 4 * PC), mode="drop")
    )
    condensed = lax.dot_general(
        cond_vectors, placed, (((0,), (0,)), ((), ())), preferred_element_type=jnp.float32
    )
    return condensed.astype(jnp.bfloat16).reshape(1, 1, NC, 4 * PC)


def solution(mesh):
    return jax.shard_map(
        body,
        mesh=mesh,
        in_specs=(
            P("wide", "narrow", None),
            P("wide", "narrow", None),
            P("wide", "narrow", None),
            P("wide", "narrow"),
            P("wide", "narrow"),
            P("wide", "narrow"),
            P("narrow", None),
        ),
        out_specs=P("wide", "narrow", None, None),
        check_vma=False,
    )
```

profile of v0, /device:TPU:1, one launch (start us, length us, event | category | flops | bytes accessed | tf_op | source)
XLA Modules:
  0.0 748.8 jit_solution(6269135097737931937)
XLA Ops:
  6.5 0.0 copy-start
  6.5 0.0 all-reduce.3.cloned.1.call-start
  6.5 1.9 broadcast_select_fusion.1
  8.5 0.0 all-reduce.3.cloned.1.call-update
  8.5 0.0 all-gather.3.cloned.1.call-start
  8.5 532.3 %all-reduce.3.cloned.1.call-done = (bf16[1,1024,128]{2,1,0:T(8,128)(2,1)}, bf16[1,1024,128]{2,1,0:T(8,128)(2,1)}) async-done(((bf16[1,1024,128]{2,1,0:T(8,128)(2,1)}, bf16[1,1024,128]{2,1,0:T(8,128)(2,1)}), (bf16[1,1024,128]{2,1,0:T(8,128)(2,1)}, bf16[1,1024,128]{2,1,0:T(8,128)(2,1)})) %all-reduce.3.cloned.1.call-update) | async-done | bytes 524304 | tf_op jit(solution)/shard_map/psum | solution.py:15
  540.8 0.0 all-gather.3.cloned.1.call-update
  540.9 0.0 all-gather.5.cloned.1.call-start
  540.9 0.7 all-gather.5.cloned.1.call-update
  541.6 0.7 add_select_fusion.1
  542.3 2.3 reduce-window.6
  544.6 0.3 slice_reduce_fusion
  544.8 0.2 reduce-window.9
  545.0 0.7 add_select_fusion
  545.7 0.1 add_bitcast_fusion
  545.8 0.7 compare_select_fusion.1
  546.5 0.7 multiply_reduce_fusion
  547.3 0.8 and_reduce_fusion
  548.0 4.9 scatter_custom_fusion.1
  552.9 4.0 all-to-all-start
  557.0 4.1 reshape.241
  561.0 4.8 reshape.243
  565.8 35.7 %all-gather.3.cloned.1.call-done = bf16[1,8192,128]{2,1,0:T(8,128)(2,1)} async-done(((bf16[1,1024,128]{2,1,0:T(8,128)(2,1)}), bf16[1,8192,128]{2,1,0:T(8,128)(2,1)}) %all-gather.3.cloned.1.call-update) | async-done | bytes 2097168 | tf_op jit(solution)/shard_map/all_gather | solution.py:33
  601.5 4.1 gather_fusion
  605.6 5.6 fusion.54
  611.2 3.0 fusion.55
  614.3 48.6 %all-gather.5.cloned.1.call-done = bf16[1,8192,128]{2,1,0:T(8,128)(2,1)} async-done(((bf16[1,1024,128]{2,1,0:T(8,128)(2,1)}), bf16[1,8192,128]{2,1,0:T(8,128)(2,1)}) %all-gather.5.cloned.1.call-update) | async-done | bytes 2097168 | tf_op jit(solution)/shard_map/all_gather | solution.py:33
  662.9 4.0 gather_fusion.1
  667.0 3.4 fusion.56
  670.4 0.5 copy-done.3
  670.9 0.8 fusion.57
  671.7 0.4 slice-done.2
  672.1 1.6 slice-done.3
  673.8 4.5 fusion.13
  678.3 4.7 fusion.16
  683.1 4.5 fusion.19
  687.6 4.5 fusion.22
  692.1 0.1 copy.9
  692.2 0.1 copy.10
  692.3 0.1 copy.11
  692.3 0.1 copy.12
  692.4 7.0 scatter_custom_fusion.2
  699.4 0.0 all-to-all-done
  699.4 4.3 all-to-all-start.1
  703.8 26.1 %all-to-all-done.1 = bf16[8,256,512]{2,1,0:T(8,128)(2,1)} async-done(((bf16[8,256,512]{2,1,0:T(8,128)(2,1)}), bf16[8,256,512]{2,1,0:T(8,128)(2,1)}, u32[]{:S(2)}, u32[]{:S(2)}) %all-to-all-start.1) | async-done | bytes 2097184 | tf_op jit(solution)/shard_map/all_to_all | solution.py:58
  729.9 10.2 %scatter_custom_fusion = bf16[1024,512]{1,0:T(8,128)(2,1)S(1)} fusion(s32[2048]{0:T(1024)S(1)} %bitcast.105, bf16[2048,512]{1,0:T(8,128)(2,1)} %bitcast.24, bf16[]{:T(256)} %constant.46.clone.1), kind=kCustom, calls=%fused_computation.32 | custom fusion | bytes 1049088 | tf_op jit(solution)/shard_map/scatter | solution.py:64
  740.1 1.0 fusion.12
  741.1 1.2 copy.13
  (29 shorter events, 0.1 us)
Async XLA Ops:
  6.5 733.6 %copy-start = (bf16[1024,768]{1,0:T(8,128)(2,1)S(1)}, bf16[1024,768]{1,0:T(8,128)(2,1)}, u32[]{:S(2)}) copy-start(bf16[1024,768]{1,0:T(8,128)(2,1)} %param.13) | copy-start | bytes 4718596
  6.5 550.4 %copy-start.5 = (bf16[1,152,4096]{2,1,0:T(8,128)(2,1)S(1)}, bf16[1,152,4096]{2,1,0:T(8,128)(2,1)}, u32[]{:S(2)}) copy-start(bf16[1,152,4096]{2,1,0:T(8,128)(2,1)} %param.8) | copy-start | bytes 3735556
  6.5 534.3 %all-reduce.3.cloned.1.call-start = ((), (), s32[]{:S(2)}) async-start(), calls=%async_computation.4 | async-start | bytes 1048576 | tf_op jit(solution)/shard_map/psum | solution.py:15
  8.5 593.0 %all-gather.3.cloned.1.call-start = ((), (), s32[]{:S(2)}) async-start(), calls=%async_computation.2 | async-start | bytes 2359296 | tf_op jit(solution)/shard_map/all_gather | solution.py:33
  540.9 122.0 %all-gather.5.cloned.1.call-start = ((), (), s32[]{:S(2)}) async-start(), calls=%async_computation.3 | async-start | bytes 2359296 | tf_op jit(solution)/shard_map/all_gather | solution.py:33
  552.9 146.5 %all-to-all-start = ((s32[8,1,256]{2,1,0:T(1,128)}), s32[8,1,256]{2,1,0:T(1,128)S(1)}, u32[]{:S(2)}, u32[]{:S(2)}) async-start(s32[8,1,256]{2,1,0:T(1,128)} %bitcast.6), calls=%async_computation | async-start | bytes 16384 | tf_op jit(solution)/shard_map/all_to_all | solution.py:59
  561.0 4.8 copy-start.7
  605.6 5.6 copy-start.1
  605.6 5.6 copy-start.4
  666.9 3.4 copy-start.2
  666.9 3.9 copy-start.3
  667.0 5.2 slice-start.2
  667.0 11.3 %slice-start = ((s8[4980736]{0:T(1024)(128)(4,1)}), s8[4194304]{0:T(1024)(128)(4,1)S(1)}, s32[]{:S(2)}) async-start(s8[4980736]{0:T(1024)(128)(4,1)} %bitcast.84), calls=%async_computation.5 | async-start | bytes 8388608
  670.9 2.9 slice-start.3
  670.9 2.9 copy-start.6
  670.9 7.4 slice-start.1
  699.4 30.5 %all-to-all-start.1 = ((bf16[8,256,512]{2,1,0:T(8,128)(2,1)}), bf16[8,256,512]{2,1,0:T(8,128)(2,1)}, u32[]{:S(2)}, u32[]{:S(2)}) async-start(bf16[8,256,512]{2,1,0:T(8,128)(2,1)} %bitcast.88), calls=%async_computation.1 | async-start | bytes 4194304 | tf_op jit(solution)/shard_map/all_to_all | solution.py:58
Sparse Core Ops, SparseCore 0:
  10.3 530.4 all-reduce.2
  543.1 58.3 all-gather.2
  603.8 59.0 all-gather.4
where the time goes:
time: 749 us
  waiting for transfers between devices  643 us (86%)
  local copies, waits for them, and re-layouts  36.4 us (5%)
  matrix products  32.2 us (4%)
  other arithmetic  15.1 us (2%)
  between operations  13.3 us (2%)
  starting transfers between devices  8.44 us (1%)
    psum x1, waiting for transfers between devices, from_root(): return lax.psum(kept, axis)  532 us
    all_gather x2, waiting for transfers between devices, body(): panel_list.append(lax.all_gather(owner_rows, 'narrow', axis=1, tiled=True))  84.3 us
    all_to_all x1, waiting for transfers between devices, body(): lax.all_to_all(send_rows, 'narrow', split_axis=0, concat_axis=0, tiled=True)  26.1 us
    dot_general x4, matrix products, body(): jnp.einsum('rs,sic->ric', selector, product, precision=lax.Precision.HIGH...  18.3 us
  transfers between devices with their start and end apart: 5, of which 4 were waited for; matrix products, arithmetic and copies ran while one was open for 9% of the time, Pallas kernels for 0%

commit v1 on v0

v1 whole, which is shorter than its diff:
```python
import jax
import jax.numpy as jnp
from jax import lax
from jax.experimental import pallas as pl
from jax.experimental.pallas import tpu as pltpu
from jax.sharding import PartitionSpec as P

BLK = 64
PC = 128
NC = 768
RB = 16
SLOTS = 152
ROWS = 1024
CAP = 256
GROUPS = 52
SORTED = GROUPS * 4
F32 = jnp.float32
BF16 = jnp.bfloat16


def iota(shape, dim):
    return lax.broadcasted_iota(jnp.int32, shape, dim)


def kernel(
    pan_in, stiff, mass, brow, bcol, imap, vec, out,
    own, other, kx, mx, vx, vt, perm, zk, zm, lhs, run, prod, sel, wts, pos_s, pos_r, send, recv,
    meta, meta_s,
    load_sem, meta_sem, a_send, a_recv, f_send, b1_send, b1_recv, b2_send, b2_recv,
    c_send, c_recv, p_send, p_recv, x_send, x_recv,
):
    w = lax.axis_index("wide")
    n = lax.axis_index("narrow")
    core = lax.rem(w, 2)
    xh = lax.rem(w // 2, 2)
    z = w // 4
    y = n // 2
    xl = lax.rem(n, 2)
    x = 2 * xh + xl

    def dev(z_, xh_, core_, n_):
        return {"wide": z_ * 4 + xh_ * 2 + core_, "narrow": n_}

    def remote(src, dst, ssem, rsem, where):
        return pltpu.make_async_remote_copy(
            src_ref=src, dst_ref=dst, send_sem=ssem, recv_sem=rsem,
            device_id=where, device_id_type=pl.DeviceIdType.MESH,
        )

    loads = [
        pltpu.make_async_copy(stiff.at[0], kx, load_sem.at[0]),
        pltpu.make_async_copy(mass.at[0], mx, load_sem.at[1]),
        pltpu.make_async_copy(vec, vx, load_sem.at[2]),
    ]
    for c in loads:
        c.start()

    def narrow_peer(d):
        return dev(z, xh, core, lax.rem(y + d // 2, 4) * 2 + lax.rem(xl + d % 2, 2))

    def x_at(xx):
        return dev(z, xx // 2, core, y * 2 + lax.rem(xx, 2))

    def y_at(yy):
        return dev(z, xh, core, yy * 2 + xl)

    sibling = dev(z, xh, 1 - core, n)
    zm4 = lax.rem(z, 4)
    is_mid = zm4 == 0
    owner = z // 8
    is_src = jnp.logical_and(lax.rem(z, 8) == 0, jnp.logical_and(xh == 0, core == 0))
    src_z = 8 * core

    def up(d):
        return dev(lax.rem(z + 16 + d, 16), xh, core, n)

    STEPS = (2, 1, -1)
    middle = dev(lax.rem(jnp.where(zm4 == 3, z + 1, z - zm4), 16), xh, core, n)

    barrier = pltpu.get_barrier_semaphore()

    def greet(where):
        pl.semaphore_signal(barrier, inc=1, device_id=where, device_id_type=pl.DeviceIdType.MESH)

    for d in range(1, 8):
        greet(narrow_peer(d))
    greet(x_at(lax.rem(x + 2, 4)))
    greet(x_at(lax.rem(jnp.where(xl == 0, x + 3, x + 1), 4)))
    greet(sibling)

    @pl.when(is_mid)
    def _():
        for d in STEPS:
            greet(up(d))

    @pl.when(jnp.logical_not(is_mid))
    def _():
        greet(middle)

    is_self = jnp.logical_and(is_src, owner == 0)

    @pl.when(is_src)
    def _():
        for k in range(4):
            for h in range(2):
                if (k, h) != (0, 0):
                    greet(dev(lax.rem(z + 4 * k, 16), h, owner, n))

        @pl.when(owner == 1)
        def _():
            greet(sibling)

    is_fed = jnp.logical_and(is_mid, jnp.logical_not(is_self))

    @pl.when(is_fed)
    def _():
        greet(dev(src_z, 0, 0, n))

    pl.semaphore_wait(
        barrier,
        10
        + jnp.where(is_mid, 3, 1)
        + jnp.where(is_src, 7 + owner, 0)
        + jnp.where(is_fed, 1, 0),
    )

    def a_rows(yy, xx):
        return pl.ds(yy * 16 + xx * 4, 4)

    def b_rows(yy, xx):
        return pl.ds(64 + xx * 16 + yy * 4, 4)

    mine_a = own.at[a_rows(y, x)]
    mine_b = own.at[b_rows(y, x)]

    @pl.when(is_src)
    def _():
        for i, rows in enumerate((a_rows, b_rows)):
            for k in (2, 1, 3, 0):
                for h in range(2):
                    src = pan_in.at[pl.ds(h * 8 + i * 4, 4)]
                    dst = own.at[rows(y, 2 * h + xl)]
                    s = a_send.at[i, k * 2 + h]
                    if (k, h) != (0, 0):
                        remote(src, dst, s, a_recv.at[i], dev(lax.rem(z + 4 * k, 16), h, owner, n)).start()
                    else:
                        @pl.when(owner == 0)
                        def _():
                            pltpu.make_async_copy(src, dst, a_recv.at[i]).start()

                        @pl.when(owner == 1)
                        def _():
                            remote(src, dst, s, a_recv.at[i], sibling).start()

    m = imap[...]
    target = lax.shift_right_logical(m, 10)
    spot = jnp.bitwise_and(m, 1023) + 1
    tri = jnp.where(iota((128, 128), 0) < iota((128, 128), 1), 1.0, 0.0).astype(BF16)
    carry = jnp.zeros((8, 1), F32)
    idx_parts = []
    for b in range(8):
        tb = target[:, b * 128 : (b + 1) * 128]
        hit = jnp.where(iota((8, 128), 0) == jnp.broadcast_to(tb, (8, 128)), 1.0, 0.0)
        before = jnp.dot(hit.astype(BF16), tri, preferred_element_type=F32) + carry
        carry = carry + jnp.sum(hit, axis=1, keepdims=True)
        rank = jnp.sum(hit * before, axis=0, keepdims=True)
        idx_parts.append(tb * CAP + rank.astype(jnp.int32))
    idx = jnp.concatenate(idx_parts, axis=1)
    spot8 = jnp.broadcast_to(spot, (8, ROWS))
    hi = lax.shift_right_logical(spot8, 5)
    lo = jnp.bitwise_and(spot8, 31)
    two = jnp.where(iota((8, ROWS), 0) == 0, hi, lo).astype(F32).astype(BF16)

    def build(g, _):
        rows = pl.ds(pl.multiple_of(g * CAP, CAP), CAP)
        s = jnp.where(iota((CAP, ROWS), 0) + g * CAP == idx, 1.0, 0.0).astype(BF16)
        sel[rows, :] = s
        t = lax.dot_general(two, s, (((1,), (1,)), ((), ())), preferred_element_type=F32)
        pos_s[g] = t
        return 0

    lax.fori_loop(0, 8, build, 0)

    pos_out = []
    for d in range(1, 8):
        to = lax.rem(y + d // 2, 4) * 2 + lax.rem(xl + d % 2, 2)
        c = remote(pos_s.at[to], pos_r.at[d], p_send.at[d], p_recv.at[d], narrow_peer(d))
        c.start()
        pos_out.append(c)
    pos_r[0] = pos_s[n]

    f_out, b1_out, b1_in = [], [], []
    fed = (
        remote(mine_a, mine_a, a_send.at[0, 0], a_recv.at[0], sibling),
        remote(mine_b, mine_b, a_send.at[1, 0], a_recv.at[1], sibling),
    )
    for i, mine in enumerate((mine_a, mine_b)):
        fed[i].wait_recv()

        @pl.when(is_mid)
        def _():
            for k, d in enumerate(STEPS):
                remote(mine, mine, f_send.at[i, k], a_recv.at[i], up(d)).start()

        for d in (2, 1, 3):
            if i == 0:
                to, came = x_at(lax.rem(x + d, 4)), own.at[a_rows(y, lax.rem(x + 4 - d, 4))]
            else:
                to, came = y_at(lax.rem(y + d, 4)), own.at[b_rows(lax.rem(y + 4 - d, 4), x)]
            c = remote(mine, mine, b1_send.at[i, d], b1_recv.at[i, d], to)
            c.start()
            b1_out.append(c)
            b1_in.append(remote(came, came, b1_send.at[i, d], b1_recv.at[i, d], to))

    br = brow[...]
    bc = bcol[...]
    sq = (SLOTS, SLOTS)
    diag = iota(sq, 0) == iota(sq, 1)
    br_b = jnp.broadcast_to(br, sq)
    brc = jnp.sum(jnp.where(diag, br_b, 0), axis=1, keepdims=True)
    bcc = jnp.sum(jnp.where(diag, jnp.broadcast_to(bc, sq), 0), axis=1, keepdims=True)
    earlier = jnp.logical_and(iota(sq, 0) < iota(sq, 1), brc == br_b)
    rank = jnp.sum(jnp.where(earlier, 1, 0), axis=0, keepdims=True)
    same = iota((RB, SLOTS), 0) == jnp.broadcast_to(br, (RB, SLOTS))
    count = jnp.sum(jnp.where(same, 1, 0), axis=1, keepdims=True)
    padded = jnp.bitwise_and(count + 3, -4)
    off = jnp.sum(jnp.where(iota((RB, SLOTS), 0) < br, padded, 0), axis=0, keepdims=True)
    dest = jnp.where(br < RB, off + rank, 4096)
    destc = jnp.sum(jnp.where(diag, jnp.broadcast_to(dest, sq), 0), axis=1, keepdims=True)
    count_l = jnp.sum(jnp.where(brc == iota((SLOTS, 128), 1), 1, 0), axis=0, keepdims=True)
    padded_l = jnp.bitwise_and(count_l + 3, -4)
    off_c = jnp.sum(jnp.where(iota((RB, 128), 1) < iota((RB, 128), 0), padded_l, 0), axis=1, keepdims=True)
    begins = jnp.logical_and(lax.shift_right_logical(off_c, 2) == iota((RB, 256), 1), count > 0)
    keep = 1 - jnp.sum(jnp.where(begins, 1, 0), axis=0, keepdims=True)
    end_l = jnp.sum(jnp.where(iota((RB, 256), 0) <= iota((RB, 256), 1), padded, 0), axis=0, keepdims=True)
    last = jnp.maximum(lax.shift_right_logical(end_l, 2) - 1, 0)
    some = jnp.minimum(count_l, 1)
    some = jnp.concatenate([some, some], axis=1)
    q = jnp.bitwise_and(bcc, 3)
    part = jnp.bitwise_and(lax.shift_right_logical(bcc, 2), 1)
    bx = 2 * jnp.bitwise_and(lax.shift_right_logical(bcc, 3), 1) + jnp.bitwise_and(lax.shift_right_logical(bcc, 4), 1)
    by = lax.shift_right_logical(bcc, 5)
    place = jnp.where(part == 1, 64 + bx * 16 + by * 4, by * 16 + bx * 4) + q
    block = jnp.sum(jnp.where(destc == iota((SLOTS, 256), 1), place, 0), axis=0, keepdims=True)
    r8 = iota((8, 256), 0)
    meta[...] = jnp.where(r8 == 0, block, jnp.where(r8 == 1, keep, jnp.where(r8 == 2, last, some)))
    to_scalar = pltpu.make_async_copy(meta, meta_s, meta_sem)
    to_scalar.start()
    perm[...] = jnp.where(iota((SORTED, SLOTS), 0) == dest, 1.0, 0.0).astype(BF16)

    for c in b1_in:
        c.wait_recv()
    row_a = own.at[pl.ds(y * 16, 16)]
    row_b = own.at[pl.ds(64 + x * 16, 16)]
    far_a = other.at[pl.ds(y * 16, 16)]
    far_b = other.at[pl.ds(64 + x * 16, 16)]
    b2_out, b2_in, c_out = [], [], []
    for d in (2, 1, 3):
        for i in range(2):
            if i == 0:
                to, o = y_at(lax.rem(y + d, 4)), lax.rem(y + 4 - d, 4) * 16
            else:
                to, o = x_at(lax.rem(x + d, 4)), 64 + lax.rem(x + 4 - d, 4) * 16
            block_ref = (row_a, row_b)[i]
            c = remote(block_ref, block_ref, b2_send.at[i, d], b2_recv.at[i, d], to)
            c.start()
            b2_out.append(c)
            came = own.at[pl.ds(o, 16)]
            b2_in.append((came, o, d, remote(came, came, b2_send.at[i, d], b2_recv.at[i, d], to)))
    for i, block_ref in enumerate((row_a, row_b)):
        c = remote(block_ref, (far_a, far_b)[i], c_send.at[i], c_recv.at[i], sibling)
        c.start()
        c_out.append(c)

    loads[0].wait()
    loads[1].wait()

    def order(j, _):
        lanes = pl.ds(pl.multiple_of(j * 512, 512), 512)
        for src, dst in ((kx, zk), (mx, zm)):
            t = jnp.dot(perm[...], src[:, lanes], preferred_element_type=F32)
            for i in range(4):
                dst[pl.ds(j * 4 + i, SORTED, stride=32), :] = t[:, i * 128 : (i + 1) * 128]
        return 0

    lax.fori_loop(0, 8, order, 0)
    left = iota((32, 128), 1) < 64

    def assemble(g, _):
        for mat, src in enumerate((zk, zm)):
            for pair in range(2):
                o = pl.multiple_of(g * 128 + pair * 64, 64)
                t0 = src[pl.ds(o, 32), :]
                t1 = src[pl.ds(o + 32, 32), :]
                even = jnp.where(left, t0, pltpu.roll(t1, 64, 1))
                odd = jnp.where(left, pltpu.roll(t0, 64, 1), t1)
                lhs[g, mat * 64 : mat * 64 + 32, pair * 128 : (pair + 1) * 128] = even.astype(BF16)
                lhs[g, mat * 64 + 32 : mat * 64 + 64, pair * 128 : (pair + 1) * 128] = odd.astype(BF16)
        return 0

    lax.fori_loop(0, GROUPS, assemble, 0)

    loads[2].wait()

    def flip(k, _):
        o = pl.ds(pl.multiple_of(k * 256, 256), 256)
        vt[:, o] = vx[o, :].T
        return 0

    lax.fori_loop(0, 4, flip, 0)
    for d in range(1, 8):
        pos_out[d - 1].wait_recv()

    def weigh(d, _):
        t = pos_r[d]
        at = (t[0:1, :] * 32.0 + t[1:2, :]).astype(jnp.int32)
        q_d = jnp.where(iota((ROWS, CAP), 0) + 1 == at, 1.0, 0.0).astype(BF16)
        wts[:, pl.ds(pl.multiple_of(d * CAP, CAP), CAP)] = jnp.dot(
            vt[...], q_d, preferred_element_type=F32
        ).astype(BF16)
        return 0

    lax.fori_loop(0, 8, weigh, 0)

    for k, (came, o, d, c) in enumerate(b2_in):
        c.wait_recv()
        h = remote(came, other.at[pl.ds(o, 16)], c_send.at[2 + k], c_recv.at[2 + k], sibling)
        h.start()
        c_out.append(h)
    to_scalar.wait()

    x_out, x_in = [], []
    for half in range(2):
        pan = (own, other)[half]
        if half == 1:
            offs = [y * 16, 64 + x * 16] + [o for _, o, _, _ in b2_in]
            for k, o in enumerate(offs):
                came = other.at[pl.ds(o, 16)]
                remote(came, came, c_send.at[k], c_recv.at[k], sibling).wait_recv()

        def multiply(g, held):
            rhs = jnp.concatenate(
                [
                    pan[meta_s[0, g * 4 + i]]
                    for i in range(4)
                ],
                axis=0,
            )
            t = jnp.dot(lhs[g], rhs, preferred_element_type=F32)
            held = t + held * meta_s[1, g].astype(F32)
            run[g] = held
            return held

        lax.fori_loop(0, GROUPS, multiply, jnp.zeros((128, PC), F32))

        def collect(r, _):
            t = run[meta_s[2, r]] * meta_s[3, r].astype(F32)
            rows = pl.ds(pl.multiple_of(r * BLK, BLK), BLK)
            prod[rows, 0:PC] = t[0:BLK].astype(BF16)
            prod[rows, PC : 2 * PC] = t[BLK : 2 * BLK].astype(BF16)
            return 0

        lax.fori_loop(0, RB, collect, 0)

        for d in (4, 5, 2, 3, 6, 7, 1, 0):
            to = lax.rem(y + d // 2, 4) * 2 + lax.rem(xl + d % 2, 2)
            rows = pl.ds(pl.multiple_of(to * CAP, CAP), CAP)
            t = jnp.dot(sel[rows, :], prod[...], preferred_element_type=F32).astype(BF16)
            if d == 0:
                recv[half, 0:CAP, :] = t
            else:
                send[half, d] = t
                c = remote(
                    send.at[half, d], recv.at[half, d * CAP : (d + 1) * CAP],
                    x_send.at[half, d], x_recv.at[half, d], narrow_peer(d),
                )
                c.start()
                x_out.append(c)

    for half in range(2):
        which = core if half == 0 else 1 - core
        for c in x_out[half * 7 : half * 7 + 7]:
            c.wait_recv()
        t = jnp.dot(wts[...], recv[half], preferred_element_type=F32)
        out[:, pl.ds(pl.multiple_of(which * 2 * PC, 2 * PC), 2 * PC)] = t.astype(BF16)

    for c in pos_out + b1_out + b2_out + c_out + x_out:
        c.wait_send()

    @pl.when(is_mid)
    def _():
        for i, mine in enumerate((mine_a, mine_b)):
            for k, d in enumerate(STEPS):
                remote(mine, mine, f_send.at[i, k], a_recv.at[i], up(d)).wait_send()

    @pl.when(is_src)
    def _():
        for i, rows in enumerate((a_rows, b_rows)):
            for k in (2, 1, 3, 0):
                for h in range(2):
                    src = pan_in.at[pl.ds(h * 8 + i * 4, 4)]
                    dst = own.at[rows(y, 2 * h + xl)]
                    s = a_send.at[i, k * 2 + h]
                    if (k, h) != (0, 0):
                        remote(src, dst, s, a_recv.at[i], dev(lax.rem(z + 4 * k, 16), h, owner, n)).wait_send()
                    else:
                        @pl.when(owner == 1)
                        def _():
                            remote(src, dst, s, a_recv.at[i], sibling).wait_send()


def body(panels, stiff_blocks, mass_blocks, block_rows, block_cols, interface_map, cond_vectors):
    places = interface_map.reshape(RB, 32, 2).transpose(0, 2, 1).reshape(1, ROWS)
    hbm = pl.BlockSpec(memory_space=pl.ANY)
    vmem = pl.BlockSpec(memory_space=pltpu.VMEM)
    dma = pltpu.SemaphoreType.DMA
    res = pl.pallas_call(
        kernel,
        out_shape=jax.ShapeDtypeStruct((NC, 4 * PC), BF16),
        in_specs=[hbm, hbm, hbm, vmem, vmem, vmem, hbm],
        out_specs=vmem,
        scratch_shapes=[
            pltpu.VMEM((128, BLK, PC), BF16),
            pltpu.VMEM((128, BLK, PC), BF16),
            pltpu.VMEM((SLOTS, BLK * BLK), BF16),
            pltpu.VMEM((SLOTS, BLK * BLK), BF16),
            pltpu.VMEM((ROWS, NC), BF16),
            pltpu.VMEM((NC, ROWS), BF16),
            pltpu.VMEM((SORTED, SLOTS), BF16),
            pltpu.VMEM((SORTED * 32, 128), F32),
            pltpu.VMEM((SORTED * 32, 128), F32),
            pltpu.VMEM((GROUPS, 128, 256), BF16),
            pltpu.VMEM((GROUPS, 128, PC), F32),
            pltpu.VMEM((ROWS, 2 * PC), BF16),
            pltpu.VMEM((8 * CAP, ROWS), BF16),
            pltpu.VMEM((NC, 8 * CAP), BF16),
            pltpu.VMEM((8, 8, CAP), F32),
            pltpu.VMEM((8, 8, CAP), F32),
            pltpu.VMEM((2, 8, CAP, 2 * PC), BF16),
            pltpu.VMEM((2, 8 * CAP, 2 * PC), BF16),
            pltpu.VMEM((8, 256), jnp.int32),
            pltpu.SMEM((8, 256), jnp.int32),
            dma((3,)), dma, dma((2, 8)), dma((2,)), dma((2, 3)), dma((2, 4)), dma((2, 4)), dma((2, 4)), dma((2, 4)),
            dma((8,)), dma((8,)), dma((8,)), dma((8,)), dma((2, 8)), dma((2, 8)),
        ],
        compiler_params=pltpu.CompilerParams(
            collective_id=0, has_side_effects=True, vmem_limit_bytes=60 * 2**20
        ),
    )(panels.reshape(RB, BLK, PC), stiff_blocks, mass_blocks, block_rows, block_cols, places, cond_vectors)
    return res.reshape(1, 1, NC, 4 * PC)


def solution(mesh):
    return jax.shard_map(
        body,
        mesh=mesh,
        in_specs=(
            P("wide", "narrow", None),
            P("wide", "narrow", None),
            P("wide", "narrow", None),
            P("wide", "narrow"),
            P("wide", "narrow"),
            P("wide", "narrow"),
            P("narrow", None),
        ),
        out_specs=P("wide", "narrow", None, None),
        check_vma=False,
    )
```

time: 749 us -> 96.2 us (0.13)
  the two profiles are of different devices: /device:TPU:1 before, /device:TPU:33 now
where the time goes in v1:
time: 96.2 us; the launch traced here: 95.9 us
  Pallas kernels  90.9 us (94%)
  local copies, waits for them, and re-layouts  3.63 us (4%)
  other arithmetic  1.35 us (1%)
    pallas_call x1, Pallas kernels, body(): pl.pallas_call(kernel, out_shape=jax.ShapeDtypeStruct((NC, 4 * PC), BF16)...  90.9 us
    unnamed x2, local copies, waits for them, and re-layouts  2.57 us

profile of v1, /device:TPU:33, one launch (start us, length us, event | category | flops | bytes accessed | tf_op | source)
XLA Modules:
  0.0 95.9 jit_solution(10867058275393311811)
XLA Ops:
  0.0 0.5 broadcast.3
  0.5 1.3 %reduce.3 = s32[1024]{0:T(1024)S(1)} reduce(s32[1,1024]{1,0:T(1,128)} %param.12, s32[]{:T(128)} %broadcast.3), dimensions={0}, to_apply=%param.12.reduce_sub_computation.3 | reduce | bytes 8196 | tf_op args[5]
  1.9 0.2 reshape.13
  2.1 0.2 copy.9
  2.2 0.7 reshape.14.imap
  2.9 90.9 %shard_map.73 = bf16[768,512]{1,0:T(8,128)(2,1)} custom-call(bf16[16,64,128]{2,1,0:T(8,128)(2,1)} %bitcast.5, bf16[1,152,4096]{2,1,0:T(8,128)(2,1)} %stiff.1, bf16[1,152,4096]{2,1,0:T(8,128)(2,1)} %mass.1, s32[1,152]{1,0:T(1,128)} %brow.1, s32[1,152]{1,0:T(1,128)} %bcol.1, s32[1,1024]{1,0:T(1,128)} %reshape.14.imap, bf16[1024,768]{1,0:T(8,128)(2,1)} %vec.1), custom_call_target="tpu_custom_call" | custom-call | tf_op jit(solution)/shard_map/pallas_call | solution.py:417
  93.9 2.1 %copy.11 = bf16[1,1,768,512]{3,2,1,0:T(8,128)(2,1)} copy(bf16[1,1,768,512]{3,2,1,0:T(8,128)(2,1)} %bitcast.3) | data formatting | bytes 1572864

commit v2 on v1

--- a/solution.py
+++ b/solution.py
@@ -97,31 +97,35 @@
     def _():
         greet(middle)
 
-    is_self = jnp.logical_and(is_src, owner == 0)
-
-    @pl.when(is_src)
-    def _():
-        for k in range(4):
-            for h in range(2):
-                if (k, h) != (0, 0):
-                    greet(dev(lax.rem(z + 4 * k, 16), h, owner, n))
-
-        @pl.when(owner == 1)
-        def _():
-            greet(sibling)
-
-    is_fed = jnp.logical_and(is_mid, jnp.logical_not(is_self))
+    is_root = jnp.logical_and(z == src_z, xh == 1)
+    feeds = jnp.logical_or(is_src, is_root)
+    is_fed = jnp.logical_and(is_mid, z != src_z)
+    crosses = jnp.logical_and(z == 8, core == xh)
+    across = dev(z, 1 - xh, 1 - core, 2 * y + 1 - xl)
+
+    def fed_plane(k):
+        return dev(lax.rem(z + 4 * k, 16), xh, owner, n)
+
+    @pl.when(feeds)
+    def _():
+        for k in range(1, 4):
+            greet(fed_plane(k))
 
     @pl.when(is_fed)
     def _():
-        greet(dev(src_z, 0, 0, n))
+        greet(dev(src_z, xh, core * xh, n))
+
+    @pl.when(crosses)
+    def _():
+        greet(across)
 
     pl.semaphore_wait(
         barrier,
         10
         + jnp.where(is_mid, 3, 1)
-        + jnp.where(is_src, 7 + owner, 0)
-        + jnp.where(is_fed, 1, 0),
+        + jnp.where(feeds, 3, 0)
+        + jnp.where(is_fed, 1, 0)
+        + jnp.where(crosses, 1, 0),
     )
 
     def a_rows(yy, xx):
@@ -133,40 +137,56 @@
     mine_a = own.at[a_rows(y, x)]
     mine_b = own.at[b_rows(y, x)]
 
+    def owner_copies(i):
+        rows = (a_rows, b_rows)[i]
+        first = pan_in.at[pl.ds(i * 4, 4)]
+        second = pan_in.at[pl.ds(8 + i * 4, 4)]
+        here = own.at[rows(y, xl)]
+        there = own.at[rows(y, 3 - xl)]
+        root = dev(z, 1, owner, 2 * y + 1 - xl)
+        return (
+            [remote(second, there, a_send.at[i, 0], a_recv.at[i], root)]
+            + [remote(first, here, a_send.at[i, k], a_recv.at[i], fed_plane(k)) for k in (2, 1, 3)],
+            pltpu.make_async_copy(first, here, a_recv.at[i]),
+            remote(first, here, a_send.at[i, 4], a_recv.at[i], sibling),
+        )
+
     @pl.when(is_src)
     def _():
-        for i, rows in enumerate((a_rows, b_rows)):
-            for k in (2, 1, 3, 0):
-                for h in range(2):
-                    src = pan_in.at[pl.ds(h * 8 + i * 4, 4)]
-                    dst = own.at[rows(y, 2 * h + xl)]
-                    s = a_send.at[i, k * 2 + h]
-                    if (k, h) != (0, 0):
-                        remote(src, dst, s, a_recv.at[i], dev(lax.rem(z + 4 * k, 16), h, owner, n)).start()
-                    else:
-                        @pl.when(owner == 0)
-                        def _():
-                            pltpu.make_async_copy(src, dst, a_recv.at[i]).start()
-
-                        @pl.when(owner == 1)
-                        def _():
-                            remote(src, dst, s, a_recv.at[i], sibling).start()
-
-    m = imap[...]
-    target = lax.shift_right_logical(m, 10)
-    spot = jnp.bitwise_and(m, 1023) + 1
+        for i in range(2):
+            far, local, near = owner_copies(i)
+            for c in far:
+                c.start()
+
+            @pl.when(owner == 0)
+            def _():
+                local.start()
+
+            @pl.when(owner == 1)
+            def _():
+                near.start()
+
+    m = jnp.broadcast_to(imap[...], (8, ROWS))
+    m = jnp.where(iota((8, ROWS), 0) == 0, lax.shift_right_logical(m, 7), jnp.bitwise_and(m, 127)).astype(F32).astype(BF16)
+    lane = iota((128, 128), 1)
+    row_of = (lane // 64) * 64 + jnp.bitwise_and(lane, 31) * 2 + jnp.bitwise_and(lane // 32, 1)
+    swap = jnp.where(iota((128, 128), 0) == row_of, 1.0, 0.0).astype(BF16)
     tri = jnp.where(iota((128, 128), 0) < iota((128, 128), 1), 1.0, 0.0).astype(BF16)
     carry = jnp.zeros((8, 1), F32)
-    idx_parts = []
+    idx_parts, spot_parts = [], []
     for b in range(8):
-        tb = target[:, b * 128 : (b + 1) * 128]
+        t = jnp.dot(m[:, b * 128 : (b + 1) * 128], swap, preferred_element_type=F32).astype(jnp.int32)
+        mb = t[0:1] * 128 + t[1:2]
+        tb = lax.shift_right_logical(mb, 10)
+        spot_parts.append(jnp.bitwise_and(mb, 1023) + 1)
+        near = 2 * jnp.bitwise_and(lax.shift_right_logical(tb, 1) + 4 - y, 3) + jnp.bitwise_and(tb + xl, 1)
         hit = jnp.where(iota((8, 128), 0) == jnp.broadcast_to(tb, (8, 128)), 1.0, 0.0)
         before = jnp.dot(hit.astype(BF16), tri, preferred_element_type=F32) + carry
         carry = carry + jnp.sum(hit, axis=1, keepdims=True)
         rank = jnp.sum(hit * before, axis=0, keepdims=True)
-        idx_parts.append(tb * CAP + rank.astype(jnp.int32))
+        idx_parts.append(near * CAP + rank.astype(jnp.int32))
     idx = jnp.concatenate(idx_parts, axis=1)
-    spot8 = jnp.broadcast_to(spot, (8, ROWS))
+    spot8 = jnp.broadcast_to(jnp.concatenate(spot_parts, axis=1), (8, ROWS))
     hi = lax.shift_right_logical(spot8, 5)
     lo = jnp.bitwise_and(spot8, 31)
     two = jnp.where(iota((8, ROWS), 0) == 0, hi, lo).astype(F32).astype(BF16)
@@ -183,12 +203,19 @@
 
     pos_out = []
     for d in range(1, 8):
-        to = lax.rem(y + d // 2, 4) * 2 + lax.rem(xl + d % 2, 2)
-        c = remote(pos_s.at[to], pos_r.at[d], p_send.at[d], p_recv.at[d], narrow_peer(d))
+        c = remote(pos_s.at[d], pos_r.at[d], p_send.at[d], p_recv.at[d], narrow_peer(d))
         c.start()
         pos_out.append(c)
-    pos_r[0] = pos_s[n]
-
+    pos_r[0] = pos_s[0]
+
+    loads[2].wait()
+
+    def flip(k, _):
+        o = pl.ds(pl.multiple_of(k * 256, 256), 256)
+        vt[:, o] = vx[o, :].T
+        return 0
+
+    lax.fori_loop(0, 4, flip, 0)
     f_out, b1_out, b1_in = [], [], []
     fed = (
         remote(mine_a, mine_a, a_send.at[0, 0], a_recv.at[0], sibling),
@@ -196,6 +223,11 @@
     )
     for i, mine in enumerate((mine_a, mine_b)):
         fed[i].wait_recv()
+
+        @pl.when(is_root)
+        def _():
+            for k in (2, 1, 3):
+                remote(mine, mine, a_send.at[i, k], a_recv.at[i], fed_plane(k)).start()
 
         @pl.when(is_mid)
         def _():
@@ -238,7 +270,8 @@
     some = jnp.concatenate([some, some], axis=1)
     q = jnp.bitwise_and(bcc, 3)
     part = jnp.bitwise_and(lax.shift_right_logical(bcc, 2), 1)
-    bx = 2 * jnp.bitwise_and(lax.shift_right_logical(bcc, 3), 1) + jnp.bitwise_and(lax.shift_right_logical(bcc, 4), 1)
+    bxl = jnp.bitwise_and(lax.shift_right_logical(bcc, 4), 1)
+    bx = jnp.where(jnp.bitwise_and(bcc, 8) == 8, 3 - bxl, bxl)
     by = lax.shift_right_logical(bcc, 5)
     place = jnp.where(part == 1, 64 + bx * 16 + by * 4, by * 16 + bx * 4) + q
     block = jnp.sum(jnp.where(destc == iota((SLOTS, 256), 1), place, 0), axis=0, keepdims=True)
@@ -248,30 +281,6 @@
     to_scalar.start()
     perm[...] = jnp.where(iota((SORTED, SLOTS), 0) == dest, 1.0, 0.0).astype(BF16)
 
-    for c in b1_in:
-        c.wait_recv()
-    row_a = own.at[pl.ds(y * 16, 16)]
-    row_b = own.at[pl.ds(64 + x * 16, 16)]
-    far_a = other.at[pl.ds(y * 16, 16)]
-    far_b = other.at[pl.ds(64 + x * 16, 16)]
-    b2_out, b2_in, c_out = [], [], []
-    for d in (2, 1, 3):
-        for i in range(2):
-            if i == 0:
-                to, o = y_at(lax.rem(y + d, 4)), lax.rem(y + 4 - d, 4) * 16
-            else:
-                to, o = x_at(lax.rem(x + d, 4)), 64 + lax.rem(x + 4 - d, 4) * 16
-            block_ref = (row_a, row_b)[i]
-            c = remote(block_ref, block_ref, b2_send.at[i, d], b2_recv.at[i, d], to)
-            c.start()
-            b2_out.append(c)
-            came = own.at[pl.ds(o, 16)]
-            b2_in.append((came, o, d, remote(came, came, b2_send.at[i, d], b2_recv.at[i, d], to)))
-    for i, block_ref in enumerate((row_a, row_b)):
-        c = remote(block_ref, (far_a, far_b)[i], c_send.at[i], c_recv.at[i], sibling)
-        c.start()
-        c_out.append(c)
-
     loads[0].wait()
     loads[1].wait()
 
@@ -284,6 +293,29 @@
         return 0
 
     lax.fori_loop(0, 8, order, 0)
+    row_a = own.at[pl.ds(y * 16, 16)]
+    row_b = own.at[pl.ds(64 + x * 16, 16)]
+    far_a = other.at[pl.ds(y * 16, 16)]
+    far_b = other.at[pl.ds(64 + x * 16, 16)]
+    b2_out, b2_in, c_out = [], [], []
+    for i in range(2):
+        block_ref = (row_a, row_b)[i]
+        for c in b1_in[i * 3 : i * 3 + 3]:
+            c.wait_recv()
+        for d in (2, 1, 3):
+            if i == 0:
+                to, o = y_at(lax.rem(y + d, 4)), lax.rem(y + 4 - d, 4) * 16
+            else:
+                to, o = x_at(lax.rem(x + d, 4)), 64 + lax.rem(x + 4 - d, 4) * 16
+            c = remote(block_ref, block_ref, b2_send.at[i, d], b2_recv.at[i, d], to)
+            c.start()
+            b2_out.append(c)
+            came = own.at[pl.ds(o, 16)]
+            b2_in.append((came, o, d, remote(came, came, b2_send.at[i, d], b2_recv.at[i, d], to)))
+        c = remote(block_ref, (far_a, far_b)[i], c_send.at[i], c_recv.at[i], sibling)
+        c.start()
+        c_out.append(c)
+
     left = iota((32, 128), 1) < 64
 
     def assemble(g, _):
@@ -298,16 +330,13 @@
                 lhs[g, mat * 64 + 32 : mat * 64 + 64, pair * 128 : (pair + 1) * 128] = odd.astype(BF16)
         return 0
 
-    lax.fori_loop(0, GROUPS, assemble, 0)
-
-    loads[2].wait()
-
-    def flip(k, _):
-        o = pl.ds(pl.multiple_of(k * 256, 256), 256)
-        vt[:, o] = vx[o, :].T
-        return 0
-
-    lax.fori_loop(0, 4, flip, 0)
+    def assemble4(g4, _):
+        for u in range(4):
+            assemble(g4 * 4 + u, 0)
+        return 0
+
+    lax.fori_loop(0, GROUPS // 4, assemble4, 0)
+
     for d in range(1, 8):
         pos_out[d - 1].wait_recv()
 
@@ -329,7 +358,7 @@
         c_out.append(h)
     to_scalar.wait()
 
-    x_out, x_in = [], []
+    x_out = []
     for half in range(2):
         pan = (own, other)[half]
         if half == 1:
@@ -338,20 +367,16 @@
                 came = other.at[pl.ds(o, 16)]
                 remote(came, came, c_send.at[k], c_recv.at[k], sibling).wait_recv()
 
-        def multiply(g, held):
-            rhs = jnp.concatenate(
-                [
-                    pan[meta_s[0, g * 4 + i]]
-                    for i in range(4)
-                ],
-                axis=0,
-            )
-            t = jnp.dot(lhs[g], rhs, preferred_element_type=F32)
-            held = t + held * meta_s[1, g].astype(F32)
-            run[g] = held
+        def multiply(g4, held):
+            for u in range(4):
+                g = g4 * 4 + u
+                rhs = jnp.concatenate([pan[meta_s[0, g * 4 + i]] for i in range(4)], axis=0)
+                t = jnp.dot(lhs[g], rhs, preferred_element_type=F32)
+                held = t + held * meta_s[1, g].astype(F32)
+                run[g] = held
             return held
 
-        lax.fori_loop(0, GROUPS, multiply, jnp.zeros((128, PC), F32))
+        lax.fori_loop(0, GROUPS // 4, multiply, jnp.zeros((128, PC), F32))
 
         def collect(r, _):
             t = run[meta_s[2, r]] * meta_s[3, r].astype(F32)
@@ -362,20 +387,21 @@
 
         lax.fori_loop(0, RB, collect, 0)
 
-        for d in (4, 5, 2, 3, 6, 7, 1, 0):
-            to = lax.rem(y + d // 2, 4) * 2 + lax.rem(xl + d % 2, 2)
-            rows = pl.ds(pl.multiple_of(to * CAP, CAP), CAP)
+        for first in (4, 0):
+            rows = pl.ds(first * CAP, 4 * CAP)
             t = jnp.dot(sel[rows, :], prod[...], preferred_element_type=F32).astype(BF16)
-            if d == 0:
-                recv[half, 0:CAP, :] = t
-            else:
-                send[half, d] = t
-                c = remote(
-                    send.at[half, d], recv.at[half, d * CAP : (d + 1) * CAP],
-                    x_send.at[half, d], x_recv.at[half, d], narrow_peer(d),
-                )
-                c.start()
-                x_out.append(c)
+            for d in range(first, first + 4):
+                td = t[(d - first) * CAP : (d - first + 1) * CAP]
+                if d == 0:
+                    recv[half, 0:CAP, :] = td
+                else:
+                    send[half, d] = td
+                    c = remote(
+                        send.at[half, d], recv.at[half, d * CAP : (d + 1) * CAP],
+                        x_send.at[half, d], x_recv.at[half, d], narrow_peer(d),
+                    )
+                    c.start()
+                    x_out.append(c)
 
     for half in range(2):
         which = core if half == 0 else 1 - core
@@ -393,24 +419,25 @@
             for k, d in enumerate(STEPS):
                 remote(mine, mine, f_send.at[i, k], a_recv.at[i], up(d)).wait_send()
 
+    @pl.when(is_root)
+    def _():
+        for i, mine in enumerate((mine_a, mine_b)):
+            for k in (2, 1, 3):
+                remote(mine, mine, a_send.at[i, k], a_recv.at[i], fed_plane(k)).wait_send()
+
     @pl.when(is_src)
     def _():
-        for i, rows in enumerate((a_rows, b_rows)):
-            for k in (2, 1, 3, 0):
-                for h in range(2):
-                    src = pan_in.at[pl.ds(h * 8 + i * 4, 4)]
-                    dst = own.at[rows(y, 2 * h + xl)]
-                    s = a_send.at[i, k * 2 + h]
-                    if (k, h) != (0, 0):
-                        remote(src, dst, s, a_recv.at[i], dev(lax.rem(z + 4 * k, 16), h, owner, n)).wait_send()
-                    else:
-                        @pl.when(owner == 1)
-                        def _():
-                            remote(src, dst, s, a_recv.at[i], sibling).wait_send()
+        for i in range(2):
+            far, local, near = owner_copies(i)
+            for c in far:
+                c.wait_send()
+
+            @pl.when(owner == 1)
+            def _():
+                near.wait_send()
 
 
 def body(panels, stiff_blocks, mass_blocks, block_rows, block_cols, interface_map, cond_vectors):
-    places = interface_map.reshape(RB, 32, 2).transpose(0, 2, 1).reshape(1, ROWS)
     hbm = pl.BlockSpec(memory_space=pl.ANY)
     vmem = pl.BlockSpec(memory_space=pltpu.VMEM)
     dma = pltpu.SemaphoreType.DMA
@@ -446,7 +473,7 @@
         compiler_params=pltpu.CompilerParams(
             collective_id=0, has_side_effects=True, vmem_limit_bytes=60 * 2**20
         ),
-    )(panels.reshape(RB, BLK, PC), stiff_blocks, mass_blocks, block_rows, block_cols, places, cond_vectors)
+    )(panels.reshape(RB, BLK, PC), stiff_blocks, mass_blocks, block_rows, block_cols, interface_map, cond_vectors)
     return res.reshape(1, 1, NC, 4 * PC)
 
 

time: 96.2 us -> 85.6 us (0.89)
  the two profiles are of different devices: /device:TPU:33 before, /device:TPU:34 now
where the time goes in v2:
time: 85.6 us; the launch traced here: 85.4 us
  Pallas kernels  83.4 us (97%)
  local copies, waits for them, and re-layouts  2.06 us (2%)
    pallas_call x1, Pallas kernels, body(): pl.pallas_call(kernel, out_shape=jax.ShapeDtypeStruct((NC, 4 * PC), BF16)...  83.4 us
    unnamed x1, local copies, waits for them, and re-layouts  2.06 us

profile of v2, /device:TPU:34, one launch (start us, length us, event | category | flops | bytes accessed | tf_op | source)
XLA Modules:
  0.0 85.4 jit_solution(8888804378115507761)
XLA Ops:
  0.0 83.4 %shard_map.73 = bf16[768,512]{1,0:T(8,128)(2,1)} custom-call(bf16[16,64,128]{2,1,0:T(8,128)(2,1)} %bitcast.3, bf16[1,152,4096]{2,1,0:T(8,128)(2,1)} %stiff.1, bf16[1,152,4096]{2,1,0:T(8,128)(2,1)} %mass.1, s32[1,152]{1,0:T(1,128)} %brow.1, s32[1,152]{1,0:T(1,128)} %bcol.1, s32[1,1024]{1,0:T(1,128)} %imap.1, bf16[1024,768]{1,0:T(8,128)(2,1)} %vec.1), custom_call_target="tpu_custom_call" | custom-call | tf_op jit(solution)/shard_map/pallas_call | solution.py:444
  83.4 2.1 %copy.9 = bf16[1,1,768,512]{3,2,1,0:T(8,128)(2,1)} copy(bf16[1,1,768,512]{3,2,1,0:T(8,128)(2,1)} %bitcast.2) | data formatting | bytes 1572864

commit v3 on v2

--- a/solution.py
+++ b/solution.py
@@ -24,7 +24,7 @@
 
 def kernel(
     pan_in, stiff, mass, brow, bcol, imap, vec, out,
-    own, other, kx, mx, vx, vt, perm, zk, zm, lhs, run, prod, sel, wts, pos_s, pos_r, send, recv,
+    pan_0, pan_1, kx, mx, vx, vt, perm, zk, zm, lhs, run, prod, sel, wts, pos_s, pos_r, send, recv,
     meta, meta_s,
     load_sem, meta_sem, a_send, a_recv, f_send, b1_send, b1_recv, b2_send, b2_recv,
     c_send, c_recv, p_send, p_recv, x_send, x_recv,
@@ -68,14 +68,22 @@
     zm4 = lax.rem(z, 4)
     is_mid = zm4 == 0
     owner = z // 8
-    is_src = jnp.logical_and(lax.rem(z, 8) == 0, jnp.logical_and(xh == 0, core == 0))
-    src_z = 8 * core
+    at_owner = lax.rem(z, 8) == 0
+    is_src = jnp.logical_and(at_owner, jnp.logical_and(xh == 0, core == 0))
+    is_root = jnp.logical_and(at_owner, xh == 1)
+    crosses = jnp.logical_and(is_root, core == 1)
+    pans = (pan_0, pan_1)
 
     def up(d):
         return dev(lax.rem(z + 16 + d, 16), xh, core, n)
 
     STEPS = (2, 1, -1)
     middle = dev(lax.rem(jnp.where(zm4 == 3, z + 1, z - zm4), 16), xh, core, n)
+
+    def fed_plane(k, core_):
+        return dev(lax.rem(z + 4 * k, 16), xh, core_, n)
+
+    across = 2 * y + 1 - xl
 
     barrier = pltpu.get_barrier_semaphore()
 
@@ -97,74 +105,120 @@
     def _():
         greet(middle)
 
-    is_root = jnp.logical_and(z == src_z, xh == 1)
-    feeds = jnp.logical_or(is_src, is_root)
-    is_fed = jnp.logical_and(is_mid, z != src_z)
-    crosses = jnp.logical_and(z == 8, core == xh)
-    across = dev(z, 1 - xh, 1 - core, 2 * y + 1 - xl)
-
-    def fed_plane(k):
-        return dev(lax.rem(z + 4 * k, 16), xh, owner, n)
-
-    @pl.when(feeds)
+    @pl.when(is_src)
     def _():
         for k in range(1, 4):
-            greet(fed_plane(k))
-
-    @pl.when(is_fed)
-    def _():
-        greet(dev(src_z, xh, core * xh, n))
+            greet(fed_plane(k, 0))
+            greet(fed_plane(k, 1))
+        greet(dev(z, 1, 1, across))
+
+    @pl.when(is_root)
+    def _():
+        for k in range(1, 4):
+            greet(fed_plane(k, core))
 
     @pl.when(crosses)
     def _():
-        greet(across)
+        greet(dev(z, 0, 0, across))
+
+    for p in range(2):
+        @pl.when(jnp.logical_and(is_mid, z != 8 * p))
+        def _():
+            greet(dev(8 * p, xh, core * xh, n))
 
     pl.semaphore_wait(
         barrier,
         10
         + jnp.where(is_mid, 3, 1)
-        + jnp.where(feeds, 3, 0)
-        + jnp.where(is_fed, 1, 0)
-        + jnp.where(crosses, 1, 0),
+        + jnp.where(is_src, 7, 0)
+        + jnp.where(is_root, 3, 0)
+        + jnp.where(crosses, 1, 0)
+        + jnp.where(jnp.logical_and(is_mid, z != 0), 1, 0)
+        + jnp.where(jnp.logical_and(is_mid, z != 8), 1, 0),
     )
 
-    def a_rows(yy, xx):
-        return pl.ds(yy * 16 + xx * 4, 4)
-
-    def b_rows(yy, xx):
-        return pl.ds(64 + xx * 16 + yy * 4, 4)
-
-    mine_a = own.at[a_rows(y, x)]
-    mine_b = own.at[b_rows(y, x)]
-
-    def owner_copies(i):
-        rows = (a_rows, b_rows)[i]
-        first = pan_in.at[pl.ds(i * 4, 4)]
-        second = pan_in.at[pl.ds(8 + i * 4, 4)]
-        here = own.at[rows(y, xl)]
-        there = own.at[rows(y, 3 - xl)]
-        root = dev(z, 1, owner, 2 * y + 1 - xl)
-        return (
-            [remote(second, there, a_send.at[i, 0], a_recv.at[i], root)]
-            + [remote(first, here, a_send.at[i, k], a_recv.at[i], fed_plane(k)) for k in (2, 1, 3)],
-            pltpu.make_async_copy(first, here, a_recv.at[i]),
-            remote(first, here, a_send.at[i, 4], a_recv.at[i], sibling),
-        )
-
-    @pl.when(is_src)
-    def _():
-        for i in range(2):
-            far, local, near = owner_copies(i)
-            for c in far:
+    def spot_of(core_, yy, xx):
+        return jnp.where(core_ == 0, yy * 16 + xx * 4, 64 + xx * 16 + yy * 4)
+
+    mine_at = spot_of(core, y, x)
+    line_at = jnp.where(core == 0, y * 16, 64 + x * 16)
+
+    def owner_copies(p):
+        far, near = [], []
+        for c in range(2):
+            first = pan_in.at[pl.ds(c * 4, 4)]
+            second = pan_in.at[pl.ds(8 + c * 4, 4)]
+            here = pans[p].at[pl.ds(64 * c + (y * 16 + xl * 4 if c == 0 else xl * 16 + y * 4), 4)]
+            there = pans[p].at[pl.ds(64 * c + (y * 16 + (3 - xl) * 4 if c == 0 else (3 - xl) * 16 + y * 4), 4)]
+            far.append(remote(second, there, a_send.at[c, 0], a_recv.at[p], dev(z, 1, c, across)))
+            for k in (2, 1, 3):
+                far.append(remote(first, here, a_send.at[c, k], a_recv.at[p], fed_plane(k, c)))
+            if c == 0:
+                near.append(pltpu.make_async_copy(first, here, a_recv.at[p]))
+            else:
+                far.append(remote(first, here, a_send.at[c, 4], a_recv.at[p], sibling))
+        return far, near
+
+    for p in range(2):
+        @pl.when(jnp.logical_and(is_src, owner == p))
+        def _():
+            far, near = owner_copies(p)
+            for c in near + far:
                 c.start()
 
-            @pl.when(owner == 0)
-            def _():
-                local.start()
-
-            @pl.when(owner == 1)
-            def _():
-                near.start()
+    def first_round(p, d):
+        mine = pans[p].at[pl.ds(mine_at, 4)]
+        xx, yy = lax.rem(x + 4 - d, 4), lax.rem(y + 4 - d, 4)
+        came = pans[p].at[pl.ds(jnp.where(core == 0, y * 16 + xx * 4, 64 + x * 16 + yy * 4), 4)]
+        to_x = lax.rem(x + d, 4)
+        to_w = z * 4 + jnp.where(core == 0, to_x // 2, xh) * 2 + core
+        to_n = jnp.where(core == 0, y * 2 + lax.rem(to_x, 2), lax.rem(y + d, 4) * 2 + xl)
+        sems = b1_send.at[p, d], b1_recv.at[p, d], {"wide": to_w, "narrow": to_n}
+        return remote(mine, mine, *sems), remote(came, came, *sems)
+
+    def second_round(p, d):
+        line = pans[p].at[pl.ds(line_at, 16)]
+        o = jnp.where(core == 0, lax.rem(y + 4 - d, 4) * 16, 64 + lax.rem(x + 4 - d, 4) * 16)
+        came = pans[p].at[pl.ds(o, 16)]
+        to_x = lax.rem(x + d, 4)
+        to_w = z * 4 + jnp.where(core == 1, to_x // 2, xh) * 2 + core
+        to_n = jnp.where(core == 1, y * 2 + lax.rem(to_x, 2), lax.rem(y + d, 4) * 2 + xl)
+        sems = b2_send.at[p, d], b2_recv.at[p, d], {"wide": to_w, "narrow": to_n}
+        return remote(line, line, *sems), remote(came, came, *sems)
+
+    def to_sibling(p, d):
+        a, b = lax.rem(y + 4 - d, 4) * 16, 64 + lax.rem(x + 4 - d, 4) * 16
+        gone = pans[p].at[pl.ds(jnp.where(core == 0, a, b), 16)]
+        came = pans[p].at[pl.ds(jnp.where(core == 0, b, a), 16)]
+        sems = c_send.at[p, d], c_recv.at[p, d], sibling
+        return remote(gone, gone, *sems), remote(came, came, *sems)
+
+    def pass_on(p):
+        mine = pans[p].at[pl.ds(mine_at, 4)]
+        remote(mine, mine, a_send.at[0, 0], a_recv.at[p], sibling).wait_recv()
+
+        @pl.when(jnp.logical_and(is_root, owner == p))
+        def _():
+            for k in (2, 1, 3):
+                remote(mine, mine, a_send.at[0, k], a_recv.at[p], fed_plane(k, core)).start()
+
+        @pl.when(is_mid)
+        def _():
+            for k, d in enumerate(STEPS):
+                remote(mine, mine, f_send.at[p, k], a_recv.at[p], up(d)).start()
+
+        for d in (2, 1, 3):
+            first_round(p, d)[0].start()
+
+    @pl.when(jnp.logical_and(is_mid, z == 8))
+    def _():
+        pass_on(1)
+        pass_on(0)
+
+    @pl.when(jnp.logical_and(is_mid, z != 8))
+    def _():
+        pass_on(0)
+        pass_on(1)
 
     m = jnp.broadcast_to(imap[...], (8, ROWS))
     m = jnp.where(iota((8, ROWS), 0) == 0, lax.shift_right_logical(m, 7), jnp.bitwise_and(m, 127)).astype(F32).astype(BF16)
@@ -216,34 +270,6 @@
         return 0
 
     lax.fori_loop(0, 4, flip, 0)
-    f_out, b1_out, b1_in = [], [], []
-    fed = (
-        remote(mine_a, mine_a, a_send.at[0, 0], a_recv.at[0], sibling),
-        remote(mine_b, mine_b, a_send.at[1, 0], a_recv.at[1], sibling),
-    )
-    for i, mine in enumerate((mine_a, mine_b)):
-        fed[i].wait_recv()
-
-        @pl.when(is_root)
-        def _():
-            for k in (2, 1, 3):
-                remote(mine, mine, a_send.at[i, k], a_recv.at[i], fed_plane(k)).start()
-
-        @pl.when(is_mid)
-        def _():
-            for k, d in enumerate(STEPS):
-                remote(mine, mine, f_send.at[i, k], a_recv.at[i], up(d)).start()
-
-        for d in (2, 1, 3):
-            if i == 0:
-                to, came = x_at(lax.rem(x + d, 4)), own.at[a_rows(y, lax.rem(x + 4 - d, 4))]
-            else:
-                to, came = y_at(lax.rem(y + d, 4)), own.at[b_rows(lax.rem(y + 4 - d, 4), x)]
-            c = remote(mine, mine, b1_send.at[i, d], b1_recv.at[i, d], to)
-            c.start()
-            b1_out.append(c)
-            b1_in.append(remote(came, came, b1_send.at[i, d], b1_recv.at[i, d], to))
-
     br = brow[...]
     bc = bcol[...]
     sq = (SLOTS, SLOTS)
@@ -293,29 +319,24 @@
         return 0
 
     lax.fori_loop(0, 8, order, 0)
-    row_a = own.at[pl.ds(y * 16, 16)]
-    row_b = own.at[pl.ds(64 + x * 16, 16)]
-    far_a = other.at[pl.ds(y * 16, 16)]
-    far_b = other.at[pl.ds(64 + x * 16, 16)]
-    b2_out, b2_in, c_out = [], [], []
-    for i in range(2):
-        block_ref = (row_a, row_b)[i]
-        for c in b1_in[i * 3 : i * 3 + 3]:
-            c.wait_recv()
+    @pl.when(jnp.logical_not(is_mid))
+    def _():
+        pass_on(0)
+        pass_on(1)
+
+    def begin_second(p):
         for d in (2, 1, 3):
-            if i == 0:
-                to, o = y_at(lax.rem(y + d, 4)), lax.rem(y + 4 - d, 4) * 16
-            else:
-                to, o = x_at(lax.rem(x + d, 4)), 64 + lax.rem(x + 4 - d, 4) * 16
-            c = remote(block_ref, block_ref, b2_send.at[i, d], b2_recv.at[i, d], to)
-            c.start()
-            b2_out.append(c)
-            came = own.at[pl.ds(o, 16)]
-            b2_in.append((came, o, d, remote(came, came, b2_send.at[i, d], b2_recv.at[i, d], to)))
-        c = remote(block_ref, (far_a, far_b)[i], c_send.at[i], c_recv.at[i], sibling)
-        c.start()
-        c_out.append(c)
-
+            first_round(p, d)[1].wait_recv()
+        for d in (2, 1, 3):
+            second_round(p, d)[0].start()
+        to_sibling(p, 0)[0].start()
+
+    def hand_over(p):
+        for d in (2, 1, 3):
+            second_round(p, d)[1].wait_recv()
+            to_sibling(p, d)[0].start()
+
+    begin_second(0)
     left = iota((32, 128), 1) < 64
 
     def assemble(g, _):
@@ -337,35 +358,17 @@
 
     lax.fori_loop(0, GROUPS // 4, assemble4, 0)
 
-    for d in range(1, 8):
-        pos_out[d - 1].wait_recv()
-
-    def weigh(d, _):
-        t = pos_r[d]
-        at = (t[0:1, :] * 32.0 + t[1:2, :]).astype(jnp.int32)
-        q_d = jnp.where(iota((ROWS, CAP), 0) + 1 == at, 1.0, 0.0).astype(BF16)
-        wts[:, pl.ds(pl.multiple_of(d * CAP, CAP), CAP)] = jnp.dot(
-            vt[...], q_d, preferred_element_type=F32
-        ).astype(BF16)
-        return 0
-
-    lax.fori_loop(0, 8, weigh, 0)
-
-    for k, (came, o, d, c) in enumerate(b2_in):
-        c.wait_recv()
-        h = remote(came, other.at[pl.ds(o, 16)], c_send.at[2 + k], c_recv.at[2 + k], sibling)
-        h.start()
-        c_out.append(h)
+    hand_over(0)
+    begin_second(1)
     to_scalar.wait()
 
     x_out = []
     for half in range(2):
-        pan = (own, other)[half]
+        pan = pans[half]
         if half == 1:
-            offs = [y * 16, 64 + x * 16] + [o for _, o, _, _ in b2_in]
-            for k, o in enumerate(offs):
-                came = other.at[pl.ds(o, 16)]
-                remote(came, came, c_send.at[k], c_recv.at[k], sibling).wait_recv()
+            hand_over(1)
+        for d in (0, 2, 1, 3):
+            to_sibling(half, d)[1].wait_recv()
 
         def multiply(g4, held):
             for u in range(4):
@@ -403,38 +406,52 @@
                     c.start()
                     x_out.append(c)
 
+    for d in range(1, 8):
+        pos_out[d - 1].wait_recv()
+
+    def weigh(d, _):
+        t = pos_r[d]
+        at = (t[0:1, :] * 32.0 + t[1:2, :]).astype(jnp.int32)
+        q_d = jnp.where(iota((ROWS, CAP), 0) + 1 == at, 1.0, 0.0).astype(BF16)
+        wts[:, pl.ds(pl.multiple_of(d * CAP, CAP), CAP)] = jnp.dot(
+            vt[...], q_d, preferred_element_type=F32
+        ).astype(BF16)
+        return 0
+
+    lax.fori_loop(0, 8, weigh, 0)
+
     for half in range(2):
-        which = core if half == 0 else 1 - core
         for c in x_out[half * 7 : half * 7 + 7]:
             c.wait_recv()
         t = jnp.dot(wts[...], recv[half], preferred_element_type=F32)
-        out[:, pl.ds(pl.multiple_of(which * 2 * PC, 2 * PC), 2 * PC)] = t.astype(BF16)
-
-    for c in pos_out + b1_out + b2_out + c_out + x_out:
+        out[:, half * 2 * PC : (half + 1) * 2 * PC] = t.astype(BF16)
+
+    for p in range(2):
+        for d in (2, 1, 3):
+            first_round(p, d)[0].wait_send()
+            second_round(p, d)[0].wait_send()
+        for d in range(4):
+            to_sibling(p, d)[0].wait_send()
+    for c in pos_out + x_out:
         c.wait_send()
 
-    @pl.when(is_mid)
-    def _():
-        for i, mine in enumerate((mine_a, mine_b)):
+    for p in range(2):
+        mine = pans[p].at[pl.ds(mine_at, 4)]
+
+        @pl.when(is_mid)
+        def _():
             for k, d in enumerate(STEPS):
-                remote(mine, mine, f_send.at[i, k], a_recv.at[i], up(d)).wait_send()
-
-    @pl.when(is_root)
-    def _():
-        for i, mine in enumerate((mine_a, mine_b)):
+                remote(mine, mine, f_send.at[p, k], a_recv.at[p], up(d)).wait_send()
+
+        @pl.when(jnp.logical_and(is_root, owner == p))
+        def _():
             for k in (2, 1, 3):
-                remote(mine, mine, a_send.at[i, k], a_recv.at[i], fed_plane(k)).wait_send()
-
-    @pl.when(is_src)
-    def _():
-        for i in range(2):
-            far, local, near = owner_copies(i)
-            for c in far:
+                remote(mine, mine, a_send.at[0, k], a_recv.at[p], fed_plane(k, core)).wait_send()
+
+        @pl.when(jnp.logical_and(is_src, owner == p))
+        def _():
+            for c in owner_copies(p)[0]:
                 c.wait_send()
-
-            @pl.when(owner == 1)
-            def _():
-                near.wait_send()
 
 
 def body(panels, stiff_blocks, mass_blocks, block_rows, block_cols, interface_map, cond_vectors):
@@ -468,7 +485,7 @@
             pltpu.VMEM((8, 256), jnp.int32),
             pltpu.SMEM((8, 256), jnp.int32),
             dma((3,)), dma, dma((2, 8)), dma((2,)), dma((2, 3)), dma((2, 4)), dma((2, 4)), dma((2, 4)), dma((2, 4)),
-            dma((8,)), dma((8,)), dma((8,)), dma((8,)), dma((2, 8)), dma((2, 8)),
+            dma((2, 4)), dma((2, 4)), dma((8,)), dma((8,)), dma((2, 8)), dma((2, 8)),
         ],
         compiler_params=pltpu.CompilerParams(
             collective_id=0, has_side_effects=True, vmem_limit_bytes=60 * 2**20

time: 85.6 us -> 86.7 us (1.013)
  the two profiles are of different devices: /device:TPU:34 before, /device:TPU:99 now
where the time goes in v3:
time: 86.7 us; the launch traced here: 86.5 us
  Pallas kernels  84.4 us (97%)
  local copies, waits for them, and re-layouts  2.06 us (2%)
    pallas_call x1, Pallas kernels, body(): pl.pallas_call(kernel, out_shape=jax.ShapeDtypeStruct((NC, 4 * PC), BF16)...  84.4 us
    unnamed x1, local copies, waits for them, and re-layouts  2.06 us

profile of v3, /device:TPU:99, one launch (start us, length us, event | category | flops | bytes accessed | tf_op | source)
XLA Modules:
  0.0 86.5 jit_solution(15552565803269731207)
XLA Ops:
  0.0 84.4 %shard_map.73 = bf16[768,512]{1,0:T(8,128)(2,1)} custom-call(bf16[16,64,128]{2,1,0:T(8,128)(2,1)} %bitcast.3, bf16[1,152,4096]{2,1,0:T(8,128)(2,1)} %stiff.1, bf16[1,152,4096]{2,1,0:T(8,128)(2,1)} %mass.1, s32[1,152]{1,0:T(1,128)} %brow.1, s32[1,152]{1,0:T(1,128)} %bcol.1, s32[1,1024]{1,0:T(1,128)} %imap.1, bf16[1024,768]{1,0:T(8,128)(2,1)} %vec.1), custom_call_target="tpu_custom_call" | custom-call | tf_op jit(solution)/shard_map/pallas_call | solution.py:461
  84.4 2.1 %copy.9 = bf16[1,1,768,512]{3,2,1,0:T(8,128)(2,1)} copy(bf16[1,1,768,512]{3,2,1,0:T(8,128)(2,1)} %bitcast.2) | data formatting | bytes 1572864

commit v4 on v2

--- a/solution.py
+++ b/solution.py
@@ -165,6 +165,36 @@
             @pl.when(owner == 1)
             def _():
                 near.start()
+
+    def first_round(i, d):
+        mine = (mine_a, mine_b)[i]
+        if i == 0:
+            to, came = x_at(lax.rem(x + d, 4)), own.at[a_rows(y, lax.rem(x + 4 - d, 4))]
+        else:
+            to, came = y_at(lax.rem(y + d, 4)), own.at[b_rows(lax.rem(y + 4 - d, 4), x)]
+        sems = b1_send.at[i, d], b1_recv.at[i, d], to
+        return remote(mine, mine, *sems), remote(came, came, *sems)
+
+    def pass_on():
+        for i, mine in enumerate((mine_a, mine_b)):
+            remote(mine, mine, a_send.at[i, 0], a_recv.at[i], sibling).wait_recv()
+
+            @pl.when(is_root)
+            def _():
+                for k in (2, 1, 3):
+                    remote(mine, mine, a_send.at[i, k], a_recv.at[i], fed_plane(k)).start()
+
+            @pl.when(is_mid)
+            def _():
+                for k, d in enumerate(STEPS):
+                    remote(mine, mine, f_send.at[i, k], a_recv.at[i], up(d)).start()
+
+            for d in (2, 1, 3):
+                first_round(i, d)[0].start()
+
+    @pl.when(is_mid)
+    def _():
+        pass_on()
 
     m = jnp.broadcast_to(imap[...], (8, ROWS))
     m = jnp.where(iota((8, ROWS), 0) == 0, lax.shift_right_logical(m, 7), jnp.bitwise_and(m, 127)).astype(F32).astype(BF16)
@@ -216,34 +246,6 @@
         return 0
 
     lax.fori_loop(0, 4, flip, 0)
-    f_out, b1_out, b1_in = [], [], []
-    fed = (
-        remote(mine_a, mine_a, a_send.at[0, 0], a_recv.at[0], sibling),
-        remote(mine_b, mine_b, a_send.at[1, 0], a_recv.at[1], sibling),
-    )
-    for i, mine in enumerate((mine_a, mine_b)):
-        fed[i].wait_recv()
-
-        @pl.when(is_root)
-        def _():
-            for k in (2, 1, 3):
-                remote(mine, mine, a_send.at[i, k], a_recv.at[i], fed_plane(k)).start()
-
-        @pl.when(is_mid)
-        def _():
-            for k, d in enumerate(STEPS):
-                remote(mine, mine, f_send.at[i, k], a_recv.at[i], up(d)).start()
-
-        for d in (2, 1, 3):
-            if i == 0:
-                to, came = x_at(lax.rem(x + d, 4)), own.at[a_rows(y, lax.rem(x + 4 - d, 4))]
-            else:
-                to, came = y_at(lax.rem(y + d, 4)), own.at[b_rows(lax.rem(y + 4 - d, 4), x)]
-            c = remote(mine, mine, b1_send.at[i, d], b1_recv.at[i, d], to)
-            c.start()
-            b1_out.append(c)
-            b1_in.append(remote(came, came, b1_send.at[i, d], b1_recv.at[i, d], to))
-
     br = brow[...]
     bc = bcol[...]
     sq = (SLOTS, SLOTS)
@@ -293,6 +295,10 @@
         return 0
 
     lax.fori_loop(0, 8, order, 0)
+    @pl.when(jnp.logical_not(is_mid))
+    def _():
+        pass_on()
+
     row_a = own.at[pl.ds(y * 16, 16)]
     row_b = own.at[pl.ds(64 + x * 16, 16)]
     far_a = other.at[pl.ds(y * 16, 16)]
@@ -300,8 +306,8 @@
     b2_out, b2_in, c_out = [], [], []
     for i in range(2):
         block_ref = (row_a, row_b)[i]
-        for c in b1_in[i * 3 : i * 3 + 3]:
-            c.wait_recv()
+        for d in (2, 1, 3):
+            first_round(i, d)[1].wait_recv()
         for d in (2, 1, 3):
             if i == 0:
                 to, o = y_at(lax.rem(y + d, 4)), lax.rem(y + 4 - d, 4) * 16
@@ -337,20 +343,6 @@
 
     lax.fori_loop(0, GROUPS // 4, assemble4, 0)
 
-    for d in range(1, 8):
-        pos_out[d - 1].wait_recv()
-
-    def weigh(d, _):
-        t = pos_r[d]
-        at = (t[0:1, :] * 32.0 + t[1:2, :]).astype(jnp.int32)
-        q_d = jnp.where(iota((ROWS, CAP), 0) + 1 == at, 1.0, 0.0).astype(BF16)
-        wts[:, pl.ds(pl.multiple_of(d * CAP, CAP), CAP)] = jnp.dot(
-            vt[...], q_d, preferred_element_type=F32
-        ).astype(BF16)
-        return 0
-
-    lax.fori_loop(0, 8, weigh, 0)
-
     for k, (came, o, d, c) in enumerate(b2_in):
         c.wait_recv()
         h = remote(came, other.at[pl.ds(o, 16)], c_send.at[2 + k], c_recv.at[2 + k], sibling)
@@ -368,26 +360,27 @@
                 remote(came, came, c_send.at[k], c_recv.at[k], sibling).wait_recv()
 
         def multiply(g4, held):
-            for u in range(4):
-                g = g4 * 4 + u
+            for u in range(13):
+                g = g4 * 13 + u
                 rhs = jnp.concatenate([pan[meta_s[0, g * 4 + i]] for i in range(4)], axis=0)
                 t = jnp.dot(lhs[g], rhs, preferred_element_type=F32)
                 held = t + held * meta_s[1, g].astype(F32)
                 run[g] = held
             return held
 
-        lax.fori_loop(0, GROUPS // 4, multiply, jnp.zeros((128, PC), F32))
+        lax.fori_loop(0, GROUPS // 13, multiply, jnp.zeros((128, PC), F32))
 
         def collect(r, _):
             t = run[meta_s[2, r]] * meta_s[3, r].astype(F32)
-            rows = pl.ds(pl.multiple_of(r * BLK, BLK), BLK)
+            rows = pl.ds(r * BLK, BLK)
             prod[rows, 0:PC] = t[0:BLK].astype(BF16)
             prod[rows, PC : 2 * PC] = t[BLK : 2 * BLK].astype(BF16)
             return 0
 
-        lax.fori_loop(0, RB, collect, 0)
-
-        for first in (4, 0):
+        for r in range(RB):
+            collect(r, 0)
+
+        for first in (0, 4):
             rows = pl.ds(first * CAP, 4 * CAP)
             t = jnp.dot(sel[rows, :], prod[...], preferred_element_type=F32).astype(BF16)
             for d in range(first, first + 4):
@@ -403,6 +396,20 @@
                     c.start()
                     x_out.append(c)
 
+    for d in range(1, 8):
+        pos_out[d - 1].wait_recv()
+
+    def weigh(d, _):
+        t = pos_r[d]
+        at = (t[0:1, :] * 32.0 + t[1:2, :]).astype(jnp.int32)
+        q_d = jnp.where(iota((ROWS, CAP), 0) + 1 == at, 1.0, 0.0).astype(BF16)
+        wts[:, pl.ds(pl.multiple_of(d * CAP, CAP), CAP)] = jnp.dot(
+            vt[...], q_d, preferred_element_type=F32
+        ).astype(BF16)
+        return 0
+
+    lax.fori_loop(0, 8, weigh, 0)
+
     for half in range(2):
         which = core if half == 0 else 1 - core
         for c in x_out[half * 7 : half * 7 + 7]:
@@ -410,7 +417,10 @@
         t = jnp.dot(wts[...], recv[half], preferred_element_type=F32)
         out[:, pl.ds(pl.multiple_of(which * 2 * PC, 2 * PC), 2 * PC)] = t.astype(BF16)
 
-    for c in pos_out + b1_out + b2_out + c_out + x_out:
+    for i in range(2):
+        for d in (2, 1, 3):
+            first_round(i, d)[0].wait_send()
+    for c in pos_out + b2_out + c_out + x_out:
         c.wait_send()
 
     @pl.when(is_mid)

time: 85.6 us -> 82.9 us (0.968)
  the two profiles are of different devices: /device:TPU:34 before, /device:TPU:33 now
where the time goes in v4:
time: 82.9 us; the launch traced here: 82.7 us
  Pallas kernels  80.6 us (97%)
  local copies, waits for them, and re-layouts  2.06 us (2%)
    pallas_call x1, Pallas kernels, body(): pl.pallas_call(kernel, out_shape=jax.ShapeDtypeStruct((NC, 4 * PC), BF16)...  80.6 us
    unnamed x1, local copies, waits for them, and re-layouts  2.06 us

profile of v4, /device:TPU:33, one launch (start us, length us, event | category | flops | bytes accessed | tf_op | source)
XLA Modules:
  0.0 82.7 jit_solution(2636999855131280853)
XLA Ops:
  0.0 80.6 %shard_map.73 = bf16[768,512]{1,0:T(8,128)(2,1)} custom-call(bf16[16,64,128]{2,1,0:T(8,128)(2,1)} %bitcast.3, bf16[1,152,4096]{2,1,0:T(8,128)(2,1)} %stiff.1, bf16[1,152,4096]{2,1,0:T(8,128)(2,1)} %mass.1, s32[1,152]{1,0:T(1,128)} %brow.1, s32[1,152]{1,0:T(1,128)} %bcol.1, s32[1,1024]{1,0:T(1,128)} %imap.1, bf16[1024,768]{1,0:T(8,128)(2,1)} %vec.1), custom_call_target="tpu_custom_call" | custom-call | tf_op jit(solution)/shard_map/pallas_call | solution.py:454
  80.6 2.1 %copy.9 = bf16[1,1,768,512]{3,2,1,0:T(8,128)(2,1)} copy(bf16[1,1,768,512]{3,2,1,0:T(8,128)(2,1)} %bitcast.2) | data formatting | bytes 1572864

commit v5 on v4

--- a/solution.py
+++ b/solution.py
@@ -360,15 +360,15 @@
                 remote(came, came, c_send.at[k], c_recv.at[k], sibling).wait_recv()
 
         def multiply(g4, held):
-            for u in range(13):
-                g = g4 * 13 + u
+            for u in range(26):
+                g = g4 * 26 + u
                 rhs = jnp.concatenate([pan[meta_s[0, g * 4 + i]] for i in range(4)], axis=0)
                 t = jnp.dot(lhs[g], rhs, preferred_element_type=F32)
                 held = t + held * meta_s[1, g].astype(F32)
                 run[g] = held
             return held
 
-        lax.fori_loop(0, GROUPS // 13, multiply, jnp.zeros((128, PC), F32))
+        lax.fori_loop(0, GROUPS // 26, multiply, jnp.zeros((128, PC), F32))
 
         def collect(r, _):
             t = run[meta_s[2, r]] * meta_s[3, r].astype(F32)
@@ -380,10 +380,10 @@
         for r in range(RB):
             collect(r, 0)
 
-        for first in (0, 4):
-            rows = pl.ds(first * CAP, 4 * CAP)
+        for first in (0, 2, 4, 6):
+            rows = pl.ds(first * CAP, 2 * CAP)
             t = jnp.dot(sel[rows, :], prod[...], preferred_element_type=F32).astype(BF16)
-            for d in range(first, first + 4):
+            for d in range(first, first + 2):
                 td = t[(d - first) * CAP : (d - first + 1) * CAP]
                 if d == 0:
                     recv[half, 0:CAP, :] = td
@@ -464,8 +464,8 @@
             pltpu.VMEM((ROWS, NC), BF16),
             pltpu.VMEM((NC, ROWS), BF16),
             pltpu.VMEM((SORTED, SLOTS), BF16),
-            pltpu.VMEM((SORTED * 32, 128), F32),
-            pltpu.VMEM((SORTED * 32, 128), F32),
+            pltpu.VMEM((SORTED * 32 + 32, 128), F32),
+            pltpu.VMEM((SORTED * 32 + 32, 128), F32),
             pltpu.VMEM((GROUPS, 128, 256), BF16),
             pltpu.VMEM((GROUPS, 128, PC), F32),
             pltpu.VMEM((ROWS, 2 * PC), BF16),

time: 82.9 us -> 82.4 us (level)
  no operation moved by 1% of the time
where the time goes in v5:
time: 82.4 us; the launch traced here: 82.2 us
  Pallas kernels  80.1 us (97%)
  local copies, waits for them, and re-layouts  2.06 us (2%)
    pallas_call x1, Pallas kernels, body(): pl.pallas_call(kernel, out_shape=jax.ShapeDtypeStruct((NC, 4 * PC), BF16)...  80.1 us
    unnamed x1, local copies, waits for them, and re-layouts  2.06 us

profile of v5, /device:TPU:33, one launch (start us, length us, event | category | flops | bytes accessed | tf_op | source)
XLA Modules:
  0.0 82.2 jit_solution(15038356130560737029)
XLA Ops:
  0.0 80.1 %shard_map.73 = bf16[768,512]{1,0:T(8,128)(2,1)} custom-call(bf16[16,64,128]{2,1,0:T(8,128)(2,1)} %bitcast.3, bf16[1,152,4096]{2,1,0:T(8,128)(2,1)} %stiff.1, bf16[1,152,4096]{2,1,0:T(8,128)(2,1)} %mass.1, s32[1,152]{1,0:T(1,128)} %brow.1, s32[1,152]{1,0:T(1,128)} %bcol.1, s32[1,1024]{1,0:T(1,128)} %imap.1, bf16[1024,768]{1,0:T(8,128)(2,1)} %vec.1), custom_call_target="tpu_custom_call" | custom-call | tf_op jit(solution)/shard_map/pallas_call | solution.py:454
  80.1 2.1 %copy.9 = bf16[1,1,768,512]{3,2,1,0:T(8,128)(2,1)} copy(bf16[1,1,768,512]{3,2,1,0:T(8,128)(2,1)} %bitcast.2) | data formatting | bytes 1572864
